TPU v7x, 128 devices: a whole 4x4x4 slice. The times are simulated.
128 devices in a mesh: prefix: 8 (over z_lo, y), resp: 8 (over x, core), mp: 2 (over z_hi).
Axes of the slice: x: 4, y: 4, z: 4 (z_hi: 2, z_lo: 2; z = z_hi * 2 + z_lo), core: 2. Of those that a mesh axis runs over, the one named last changes fastest.
Arguments:
- queries: bfloat16 [16, 1024, 32, 128], P('prefix', ('resp', 'mp')), may hold values from -6 to 6
- resp_keys: bfloat16 [16, 1024, 4, 128], P('prefix', ('resp', 'mp')), may hold values from -6 to 6
- resp_values: bfloat16 [16, 1024, 4, 128], P('prefix', ('resp', 'mp')), may hold values from -6 to 6
- prefix_keys: bfloat16 [2, 2048, 4, 128], P(None, 'prefix', 'mp'), may hold values from -6 to 6
- prefix_values: bfloat16 [2, 2048, 4, 128], P(None, 'prefix', 'mp'), may hold values from -6 to 6
- grad_out: bfloat16 [16, 1024, 32, 128], P('prefix', ('resp', 'mp')), may hold values from -6 to 6
- prompt_ids: int32 [16], replicated, may hold values from 0 to 1
- prefix_lengths: int32 [2], replicated, may hold values from 512 to 2048, as said below
- resp_lengths: int32 [16], replicated, may hold values from 1 to 1024, 10240 in all
Outputs:
- attention: bfloat16 [16, 1024, 32, 128], P('prefix', ('resp', 'mp'))
- d_queries: bfloat16 [16, 1024, 32, 128], P('prefix', ('resp', 'mp'))
- d_resp_keys: bfloat16 [16, 1024, 4, 128], P('prefix', ('resp', 'mp'))
- d_resp_values: bfloat16 [16, 1024, 4, 128], P('prefix', ('resp', 'mp'))
- d_prefix_keys: bfloat16 [2, 2048, 4, 128], P(None, 'prefix', 'mp')
- d_prefix_values: bfloat16 [2, 2048, 4, 128], P(None, 'prefix', 'mp')
Inputs may be any that keep to these rules, and one draw needn't show every extreme that they name: `prefix_lengths`: some prompt has all 2048 prefix positions valid. `resp_lengths`: some response has all 1024 positions valid.
All inputs are finite; a program needn't handle non-finite values.
Results may differ from a plain program's by a relative error of at most 0.04.
Values may be sent and summed in bfloat16 or wider, within the bound.
A program may use at most 192 MiB of HBM per device.

v0:
```python
import math

import jax
import jax.numpy as jnp
from jax import lax
from jax.experimental import pallas as pl
from jax.experimental.pallas import tpu as pltpu
from jax.sharding import PartitionSpec as P

HD = 128
PRE = 2048
RL = 1024
T = 128
T2 = T // 2
G = 8
R = T * G
KB = 1024
RC = 256
NT = (((1,), (1,)), ((), ()))
NN = (((1,), (0,)), ((), ()))
TN = (((0,), (0,)), ((), ()))
MESH = pl.DeviceIdType.MESH
HBM = pl.BlockSpec(memory_space=pl.ANY)
VM = pl.BlockSpec(memory_space=pltpu.VMEM)
SM = pl.BlockSpec(memory_space=pltpu.SMEM)
BF = jnp.bfloat16
F32 = jnp.float32
INV = 1.0 / math.sqrt(HD)
C2 = math.log2(math.e) / math.sqrt(HD)


def dot(a, b, dims):
    return lax.dot_general(a, b, dims, preferred_element_type=F32)


class Mover:
    def __init__(self, send, recv, local):
        self.send, self.recv, self.local, self.n, self.m = send, recv, local, 0, 0
        self.remote = []

    def to(self, src, dst, where):
        cp = pltpu.make_async_remote_copy(
            src_ref=src, dst_ref=dst, send_sem=self.send.at[self.n], recv_sem=self.recv.at[self.n],
            device_id=where, device_id_type=MESH)
        self.n += 1
        cp.start()
        self.remote.append(cp)
        return cp

    def here(self, src, dst):
        cp = pltpu.make_async_copy(src, dst, self.local.at[self.m])
        self.m += 1
        cp.start()
        return cp

    def drain(self):
        for cp in self.remote:
            cp.wait_send()


def chunks(body):
    def step(n, _):
        body(pl.multiple_of(n * RC, RC))
        return 0

    lax.fori_loop(0, R // RC, step, 0)


def fours(body):
    def step(k, _):
        body(k)
        return 0

    lax.fori_loop(0, 4, step, 0)


def got(copies):
    for cp in copies:
        cp.wait_recv()


def kernel(pid, plen_ref, rlen_ref, q, g, rk_in, rv_in, pk_in, pv_in, out, dout, fin, fr,
           qb, gb, pk0, pv0, pre1, res, S, Pm, qhl, qr, dr, mx, ls, oacc, dqacc, X, oh, dqh, ob, dqb,
           tm, far, s0, r1, s1, r2, rr1, rs, rkt, pkt, send, recv, local):
    p, r, m = lax.axis_index("prefix"), lax.axis_index("resp"), lax.axis_index("mp")
    zl, y, x, c = p // 4, p % 4, r // 2, r % 2
    sib = {"resp": x * 2 + 1 - c}
    mate = {"mp": 1 - m}
    zmate = {"prefix": (1 - zl) * 4 + y}
    xs = [{"resp": ((x + d) % 4) * 2 + c} for d in (1, 2, 3)]
    ys = [{"prefix": zl * 4 + (y + d) % 4} for d in (1, 2, 3)]
    cross = {"resp": x * 2 + 1 - c, "mp": 1 - m}
    zy = [{"prefix": ((zl + dz) % 2) * 4 + (y + d) % 4} for dz in range(2) for d in range(4)][1:]
    zx = [{"prefix": ((zl + dz) % 2) * 4 + y, "resp": ((x + d) % 4) * 2 + c} for dz in range(2) for d in range(4)][1:]
    xc = [{"resp": ((x + d) % 4) * 2 + (c + dc) % 2} for dc in range(2) for d in range(4)][1:]
    mv = Mover(send, recv, local)
    pos0 = r * T
    mine_r = r * T
    half = c * 128

    own_q = [[mv.here(s.at[b, :, pl.ds(16 * m, 16)], d.at[b, pl.ds(T2 * m, T2)]) for s, d in ((q, qb), (g, gb))] for b in range(2)]
    for kv in range(2):
        for b in range(2):
            rkt[kv, :, b] = jnp.transpose((rk_in, rv_in)[kv][b], (1, 0, 2))
            pkt[kv, :, b] = jnp.transpose((pk_in, pv_in)[kv][b], (1, 0, 2))
    rk, rv, pk, pv = rkt.at[0], rkt.at[1], pkt.at[0], pkt.at[1]
    own_r = [mv.here(s.at[pl.ds(2 * m, 2)], res.at[kv, :, :, pl.ds(mine_r + m * T2, T2)]) for kv, s in enumerate((rk, rv))]
    own_p = [mv.here(pk.at[0], pk0.at[:, zl, pl.ds(y * 256, 256)]), mv.here(pv.at[0], pv0.at[:, zl, pl.ds(y * 256, 256)]),
             mv.here(pk.at[1], pre1.at[0, :, zl, pl.ds(y * 256, 256)]), mv.here(pv.at[1], pre1.at[1, :, zl, pl.ds(y * 256, 256)])]
    peers = [mate, cross] + zy + [zx[k] for k in (4, 5, 6)] + xc
    barrier = pltpu.get_barrier_semaphore()
    for peer in peers:
        pl.semaphore_signal(barrier, inc=1, device_id=peer, device_id_type=MESH)
    pl.semaphore_wait(barrier, len(peers))

    pk_at = lambda z, yy: pk0.at[:, z, pl.ds(yy * 256 + half, 128)]
    pv_at = lambda z, yy: pv0.at[:, z, pl.ds(yy * 256 + half, 128)]
    p1_at = lambda z, yy: pre1.at[:, :, z, pl.ds(yy * 256 + half, 128)]
    r_at = (lambda xx: res.at[:, 0, 0, pl.ds(xx * 256 + half, 128)], lambda xx: res.at[:, 1, 0, pl.ds(xx * 256 + half, 128)],
            lambda xx: res.at[:, :, 1, pl.ds(xx * 256 + half, 128)])

    def swap_in(b, s, d):
        return mv.to(s.at[b, :, pl.ds(16 * (1 - m), 16)], d.at[b, pl.ds(T2 * m, T2)], mate)

    def swap_r(b):
        return [mv.to(s.at[pl.ds(2 * (1 - m), 2), b], res.at[kv, :, b, pl.ds(mine_r + m * T2, T2)], mate) for kv, s in enumerate((rk, rv))]

    def spread_y(src, at):
        return [mv.to(src, at(zl, y), w) for w in ys]

    def pass_z(cp, at):
        got(cp if isinstance(cp, list) else [cp])
        return [mv.to(at(1 - zl, y), at(1 - zl, y), w) for w in ys], [mv.to(at(1 - zl, y), at(1 - zl, y), sib)]

    def pass_y(z, cps, at):
        sent = []
        for d in (0, 2, 1):
            yy = (y + 3 - d) % 4
            got(cps[d] if isinstance(cps[d], list) else [cps[d]])
            sent.append(mv.to(at(z, yy), at(z, yy), sib))
        return sent

    def spread_r(u):
        at = r_at[u](x)
        return [mv.to(at, at, w) for w in xs], [mv.to(at, at, sib)]

    def pass_r(u, cps):
        sent = []
        for d in (0, 2, 1):
            cps[d].wait_recv()
            at = r_at[u]((x + 3 - d) % 4)
            sent.append(mv.to(at, at, sib))
        return sent

    mine_k, mine_v = pk.at[0, :, pl.ds(half, 128)], pv.at[0, :, pl.ds(half, 128)]
    mine_1 = pk.at[1, :, pl.ds(half, 128)], pv.at[1, :, pl.ds(half, 128)]
    p1_of = lambda kv: pre1.at[kv, :, zl, pl.ds(y * 256 + half, 128)]
    kz = mv.to(mine_k, pk_at(zl, y), zmate)
    ky = spread_y(mine_k, pk_at)
    vz = mv.to(mine_v, pv_at(zl, y), zmate)
    rz0 = swap_r(0)
    q_in = [swap_in(0, q, qb), None]
    pz = [mv.to(mine_1[kv], p1_of(kv), zmate) for kv in range(2)]
    g_in = [swap_in(0, g, gb), None]
    rz1 = swap_r(1)
    q_in[1], g_in[1] = swap_in(1, q, qb), swap_in(1, g, gb)
    ky2, ks = pass_z(kz, pk_at)
    vy = spread_y(mine_v, pv_at)
    vy2, vs = pass_z(vz, pv_at)
    for cp in own_r:
        cp.wait()
    got(rz0)
    rx0, rs0 = spread_r(0)
    rx1, rs1 = spread_r(1)
    py = [[mv.to(mine_1[kv], p1_of(kv), w) for kv in range(2)] for w in ys]
    ks += pass_y(zl, ky, pk_at)
    ks += pass_y(1 - zl, ky2, pk_at)
    for cp in own_q[0] + own_p:
        cp.wait()
    got([q_in[0]] + ks)

    def prefix_rows(h, kv, prompt, i):
        if h == 0:
            ref = pk0 if kv == 0 else pv0
            return ref[prompt, i]
        return pre1[kv, prompt, i]

    def limits(b, rc, resp):
        if not resp:
            return plen_ref[pid[2 * p + b]] - 1
        t = pos0 + rc // G + lax.broadcasted_iota(jnp.int32, (RC, 1), 0) // G
        return jnp.minimum(t, rlen_ref[2 * p + b] - 1)

    def head_rows(ref, b, h, rc):
        a = ref[b, pl.ds(pl.multiple_of(rc // G, RC // G), RC // G)].astype(F32)
        return a[:, h * G : (h + 1) * G].reshape(RC, HD)

    def pass_a(h, b, before_resp=None):
        prompt = pid[2 * p + b]
        @chunks
        def _(rc):
            rows = pl.ds(rc, RC)
            a = head_rows(qb, b, h, rc)
            qr[rows] = a.astype(BF)
            a = a * C2
            hi = a.astype(BF)
            qhl[rows, 0:HD] = hi
            qhl[rows, HD : 2 * HD] = (a - hi.astype(F32)).astype(BF)
        mx[...] = jnp.full_like(mx, -jnp.inf)

        def block(load, col0, base, resp):
            col = base + lax.broadcasted_iota(jnp.int32, (RC, KB), 1)

            kb = load()
            kk = jnp.concatenate([kb, kb], axis=1)
            for rc in range(0, R, RC):
                rows = pl.ds(rc, RC)
                s = dot(qhl[rows], kk, NT)
                s = jnp.where(col <= limits(b, rc, resp), s, -1e30)
                S[rows, pl.ds(col0, KB)] = s
                top = mx[rows]
                for k in range(0, KB, 128):
                    top = jnp.maximum(top, s[:, k : k + 128])
                mx[rows] = top

        def step(i, _):
            start = pl.multiple_of(i * KB, KB)
            block(lambda: prefix_rows(h, 0, prompt, i), start, start, False)
            return 0

        lax.fori_loop(0, PRE // KB, step, 0)
        if before_resp is not None:
            before_resp()
        block(lambda: res[0, h, b], PRE, 0, True)
        @chunks
        def _(rc):
            rows = pl.ds(rc, RC)
            mx[rows] = jnp.broadcast_to(jnp.max(mx[rows], axis=1, keepdims=True), (RC, 128))

    def pass_b(h, b, before_end=None):
        prompt = pid[2 * p + b]
        ls[...] = jnp.zeros_like(ls)
        oacc[...] = jnp.zeros_like(oacc)

        def block(load, col0):
            cols = pl.ds(col0, KB)

            vb = load()
            for rc in range(0, R, RC):
                rows = pl.ds(rc, RC)
                top = mx[rows]
                s = S[rows, cols]
                total = ls[rows]
                parts = []
                for k in range(0, KB, 128):
                    e = jnp.exp2(s[:, k : k + 128] - top)
                    total = total + e
                    parts.append(e.astype(BF))
                ls[rows] = total
                pb = jnp.concatenate(parts, axis=1)
                Pm[rows, cols] = pb
                oacc[rows] += dot(pb, vb, NN)

        def step(i, _):
            block(lambda: prefix_rows(h, 1, prompt, i), pl.multiple_of(i * KB, KB))
            return 0

        lax.fori_loop(0, PRE // KB, step, 0)
        block(lambda: res[1, h, b], PRE)
        if before_end is not None:
            before_end()
        @chunks
        def _(rc):
            rows = pl.ds(rc, RC)
            il = 1.0 / jnp.sum(ls[rows], axis=1, keepdims=True)
            o = (oacc[rows] * il).astype(BF).astype(F32)
            if h == 0:
                oh[b, rows] = o
            else:
                both = jnp.concatenate([oh[b, rows].reshape(RC // G, G, HD), o.reshape(RC // G, G, HD)], axis=1)
                ob[b, pl.ds(pl.multiple_of(rc // G, RC // G), RC // G)] = both.astype(BF)
            d = head_rows(gb, b, h, rc)
            t = pos0 + rc // G + lax.broadcasted_iota(jnp.int32, (RC, 1), 0) // G
            d = jnp.where(t < rlen_ref[2 * p + b], d, 0.0)
            delta = jnp.sum(d * o, axis=1, keepdims=True)
            dr[rows] = (d * il).astype(BF)
            mx[rows] = jnp.broadcast_to(delta * il, (RC, 128))

    def pass_c(h, b, hooks=()):
        prompt = pid[2 * p + b]
        if not hooks:
            dqacc[...] = jnp.zeros_like(dqacc)

        def block(load_k, load_v, col0):
            cols = pl.ds(col0, KB)
            dv = dot(dr[...], Pm[:, cols], TN).T

            vb, kb = load_v(), load_k()
            for rc in range(0, R, RC):
                rows = pl.ds(rc, RC)
                dp = dot(dr[rows], vb, NT)
                e = Pm[rows, cols].astype(F32)
                dl = mx[rows]
                ds = jnp.concatenate([e[:, k : k + 128] * (dp[:, k : k + 128] - dl) for k in range(0, KB, 128)], axis=1).astype(BF)
                Pm[rows, cols] = ds
                if not hooks:
                    dqacc[rows] += dot(ds, kb, NN)
            dk = dot(qr[...], Pm[:, cols], TN).T * INV
            return dk, dv

        def step(i, _):
            dkv = block(lambda: prefix_rows(h, 0, prompt, i), lambda: prefix_rows(h, 1, prompt, i), i * KB if isinstance(i, int) else pl.multiple_of(i * KB, KB))
            for kv in range(2):
                if b == 0:
                    X[h, kv, i] = dkv[kv]
                else:
                    before = pid[2 * p]
                    for a in range(2):
                        e = jnp.where(before == a, X[h, kv, i], 0.0) + jnp.where(prompt == a, dkv[kv], 0.0)
                        tm[h, kv, a, i] = e.astype(BF).reshape(4, 4, 64, HD)
            return 0

        if hooks:
            for i in range(PRE // KB):
                step(i, 0)
                hooks[i]()
        else:
            lax.fori_loop(0, PRE // KB, step, 0)
        dkv = block(lambda: res[0, h, b], lambda: res[1, h, b], PRE)
        for kv in range(2):
            tm[h, kv, 2, b] = dkv[kv].astype(BF).reshape(4, 4, 64, HD)
        if hooks:
            hooks[2]()
            for rc in range(0, R, RC):
                rows = pl.ds(rc, RC)
                t = dot(Pm[rows, PRE:], res[0, h, b], NN)
                for i in range(PRE // KB):
                    t = t + dot(Pm[rows, pl.ds(i * KB, KB)], prefix_rows(h, 0, prompt, i), NN)
                dqacc[rows] = t
        @chunks
        def _(rc):
            rows = pl.ds(rc, RC)
            e = dqacc[rows] * INV
            if h == 0:
                dqh[b, rows] = e
            else:
                both = jnp.concatenate([dqh[b, rows].reshape(RC // G, G, HD), e.reshape(RC // G, G, HD)], axis=1)
                dqb[b, pl.ds(pl.multiple_of(rc // G, RC // G), RC // G)] = both.astype(BF)

    ends = []

    def swap_out(b, s, d):
        ends.append(mv.to(s.at[b, pl.ds(T2 * (1 - m), T2)], d.at[b, :, pl.ds(16 * m, 16)], mate))
        owns.append(mv.here(s.at[b, pl.ds(T2 * m, T2)], d.at[b, :, pl.ds(16 * m, 16)]))

    owns = []

    def trade(h, u):
        return mv.to(tm.at[h, 1 - c, 0:2, u], far.at[h, 0:2, u], sib)

    def pair_sum(h, u, cp):
        cp.wait_recv()

        @fours
        def _(k):
            for i in range(2):
                s0[h, i, u, k] = (tm[h, c, i, u, k].astype(F32) + far[h, i, u, k].astype(F32)).astype(BF)

        return ([mv.to(s0.at[h, 0, u, :, (x + 1 + d) % 4], r1.at[h, 0, d, u], xs[d]) for d in range(3)],
                [mv.to(s0.at[h, 1, u, (y + 1 + d) % 4], r1.at[h, 1, d, u], ys[d]) for d in range(3)])

    def second(h, cps):
        sent = []
        for a in range(2):
            for j in range(2):
                got(cps[j][a])

                @fours
                def _(k):
                    t = (s0[h, 0, j, k, x] if a == 0 else s0[h, 1, j, y, k]).astype(F32)
                    for d in range(3):
                        t = t + r1[h, a, d, j, k].astype(F32)
                    s1[h, a, j, k] = t.astype(BF)

            at = y if a == 0 else x
            for n in range(1, 8):
                sent.append(mv.to(s1.at[h, a, (zl + n // 4) % 2, (at + n % 4) % 4], r2.at[h, a, n - 1], (zy if a == 0 else zx)[n - 1]))
        return sent

    def final(h, cps):
        got(cps)
        for a in range(2):
            t = s1[h, a, zl, y if a == 0 else x].astype(F32)
            for n in range(7):
                t = t + r2[h, a, n].astype(F32)
            fin[c, h, a, x] = t.astype(BF)
        at = fin.at[c, h, :, x]
        ends.extend([mv.to(at, at, w) for w in xc])

    def trade_r(h, b):
        return mv.to(tm.at[h, 1 - c, 2, b], far.at[h, 2, b], sib)

    def pair_sum_r(h, b, cp):
        cp.wait_recv()

        @fours
        def _(k):
            s0[h, 2, b, k] = (tm[h, c, 2, b, k].astype(F32) + far[h, 2, b, k].astype(F32)).astype(BF)
        return [mv.to(s0.at[h, 2, b, (x + 1 + d) % 4], rr1.at[h, d, b], xs[d]) for d in range(3)]

    def final_r(h, b, cps):
        got(cps)

        @fours
        def _(k):
            t = s0[h, 2, b, x, k].astype(F32)
            for d in range(3):
                t = t + rr1[h, d, b, k].astype(F32)
            rs[h, b, k] = t.astype(BF)

        at = fr.at[c, 2 * m + h, b]
        owns.append(mv.here(rs.at[h, b, 2 * c + m], at))
        for core, part, w in ((1 - c, m, sib), (c, 1 - m, mate), (1 - c, 1 - m, cross)):
            ends.append(mv.to(rs.at[h, b, 2 * core + part], at, w))

    later = {}

    def resp_here():
        later["y"] = pass_z(pz, p1_at)
        vs.extend(pass_y(zl, vy, pv_at))
        got(rs0 + pass_r(0, rx0))

    pass_a(0, 0, resp_here)
    py2, ps = later["y"]
    vs += pass_y(1 - zl, vy2, pv_at)
    rs1 += pass_r(1, rx1)
    got(vs)
    pass_b(0, 0, lambda: got([g_in[0]]))
    ps += pass_y(zl, py, p1_at)
    got(rz1)
    rx2, rs2 = spread_r(2)
    pass_c(0, 0)
    t00 = trade_r(0, 0)
    ps += pass_y(1 - zl, py2, p1_at)
    got(ps + rs1)
    pass_a(1, 0)
    t00 = pair_sum_r(0, 0, t00)
    rs2 += pass_r(2, rx2)
    pass_b(1, 0)
    swap_out(0, ob, out)
    pass_c(1, 0)
    t10 = trade_r(1, 0)
    swap_out(0, dqb, dout)
    final_r(0, 0, t00)
    for cp in own_q[1]:
        cp.wait()
    got(q_in[1:] + g_in[1:] + rs2)
    pass_a(0, 1)
    t10 = pair_sum_r(1, 0, t10)
    pass_b(0, 1)
    pass_c(0, 1)
    a0 = [trade(0, 0), trade(0, 1)]
    t01 = trade_r(0, 1)
    final_r(1, 0, t10)
    pass_a(1, 1)
    a0 = [pair_sum(0, u, a0[u]) for u in range(2)]
    t01 = pair_sum_r(0, 1, t01)
    pass_b(1, 1)
    swap_out(1, ob, out)
    b0 = second(0, a0)
    t11, a1 = [None], [None, None]

    def after_first():
        a1[0] = trade(1, 0)
        final_r(0, 1, t01)

    def after_second():
        a1[1] = trade(1, 1)
        a1[0] = pair_sum(1, 0, a1[0])

    def after_resp():
        t11[0] = trade_r(1, 1)
        a1[1] = pair_sum(1, 1, a1[1])

    pass_c(1, 1, (after_first, after_second, after_resp))
    swap_out(1, dqb, dout)
    t11 = pair_sum_r(1, 1, t11[0])
    final(0, b0)
    b1 = second(1, a1)
    final_r(1, 1, t11)
    final(1, b1)
    got(ends)
    for cp in owns:
        cp.wait()
    mv.drain()


def fused(pid, plens, rlens, q, g, rk, rv, pk, pv):
    v = pltpu.VMEM
    n = 200
    return pl.pallas_call(
        kernel,
        out_shape=[jax.ShapeDtypeStruct((2, T2, 32, HD), BF)] * 2
        + [jax.ShapeDtypeStruct((2, 2, 2, 4, 64, HD), BF), jax.ShapeDtypeStruct((2, 4, 2, 64, HD), BF)],
        in_specs=[SM] * 3 + [HBM] * 2 + [VM] * 4,
        out_specs=[HBM, HBM, VM, VM],
        scratch_shapes=[
            v((2, T, 16, HD), BF), v((2, T, 16, HD), BF),
            v((2, 2, 1024, HD), BF), v((2, 2, 1024, HD), BF), v((2, 2, 2, 1024, HD), BF), v((2, 2, 2, 1024, HD), BF),
            v((R, PRE + RL), F32), v((R, PRE + RL), BF),
            v((R, 2 * HD), BF), v((R, HD), BF), v((R, HD), BF),
            v((R, 128), F32), v((R, 128), F32), v((R, HD), F32), v((R, HD), F32),
            v((2, 2, 2, 1024, HD), F32), v((2, R, HD), F32), v((2, R, HD), F32), v((2, T, 16, HD), BF), v((2, T, 16, HD), BF),
            v((2, 2, 3, 2, 4, 4, 64, HD), BF), v((2, 3, 2, 4, 4, 64, HD), BF), v((2, 3, 2, 4, 4, 64, HD), BF),
            v((2, 2, 3, 2, 4, 64, HD), BF), v((2, 2, 2, 4, 64, HD), BF),
            v((2, 2, 7, 64, HD), BF), v((2, 3, 2, 4, 64, HD), BF), v((2, 2, 4, 64, HD), BF),
            v((2, 4, 2, 64, HD), BF), v((2, 2, 2, 256, HD), BF),
            pltpu.SemaphoreType.DMA((n,)), pltpu.SemaphoreType.DMA((n,)), pltpu.SemaphoreType.DMA((32,)),
        ],
        compiler_params=pltpu.CompilerParams(collective_id=1, has_side_effects=True, vmem_limit_bytes=62 * 2**20),
    )(pid, plens, rlens, q, g, rk, rv, pk, pv)


def finish_kernel(out, dout, fin, fr, out2, dout2, dpk, dpv, drk, drv):
    out2[...] = out[...]
    dout2[...] = dout[...]
    for kv, (dp, dr) in enumerate(((dpk, drk), (dpv, drv))):
        for i in range(2):
            dp[i] = jnp.transpose(fin[kv, :, i], (1, 0, 2))
            dr[i] = jnp.transpose(fr[kv, :, i], (1, 0, 2))


def finish(out, dout, fin, fr):
    rows = jax.ShapeDtypeStruct((2, T2, 32, HD), BF)
    return pl.pallas_call(
        finish_kernel,
        out_shape=[rows] * 2 + [jax.ShapeDtypeStruct((2, 256, 2, HD), BF)] * 2 + [jax.ShapeDtypeStruct((2, T2, 4, HD), BF)] * 2,
        in_specs=[VM] * 4,
        out_specs=[VM] * 6,
        compiler_params=pltpu.CompilerParams(vmem_limit_bytes=60 * 2**20),
    )(out, dout, fin, fr)


def per_device(queries, resp_keys, resp_values, prefix_keys, prefix_values, grad_out, prompt_ids, prefix_lengths, resp_lengths):
    out, dout, fin, fr = fused(prompt_ids, prefix_lengths, resp_lengths, queries, grad_out, resp_keys, resp_values, prefix_keys, prefix_values)
    attention, d_queries, dpk, dpv, drk, drv = finish(out, dout, fin.reshape(2, 2, 2, 256, HD), fr)
    return (attention, d_queries, drk, drv, dpk, dpv)


def solution(mesh):
    rows = P("prefix", ("resp", "mp"), None, None)
    pre = P(None, "prefix", "mp", None)
    return jax.shard_map(
        per_device,
        mesh=mesh,
        in_specs=(rows, rows, rows, pre, pre, rows, P(), P(), P()),
        out_specs=(rows, rows, rows, rows, pre, pre),
        check_vma=False,
    )
```

profile of v0, /device:TPU:1, one launch (start us, length us, event | category | flops | bytes accessed | tf_op | source)
XLA Modules:
  0.0 111.5 jit_solution(3082224451268396901)
XLA Ops:
  0.6 107.4 %shard_map.136 = (bf16[2,64,32,128]{3,2,1,0:T(8,128)(2,1)}, bf16[2,64,32,128]{3,2,1,0:T(8,128)(2,1)}, bf16[2,2,2,4,64,128]{5,4,3,2,1,0:T(8,128)(2,1)}, bf16[2,4,2,64,128]{4,3,2,1,0:T(8,128)(2,1)}) custom-call(s32[16]{0:T(128)} %pid.1, s32[2]{0:T(128)} %plen_ref.1, s32[16]{0:T(128)} %rlen_ref.1, bf16[2,64,32,128]{3,2,1,0:T(8,128)(2,1)} %q.1, ...), custom_call_target="tpu_custom_call" | custom-call | tf_op jit(solution)/shard_map/pallas_call | solution.py:501
  108.1 3.4 %shard_map.137 = (bf16[2,64,32,128]{3,2,1,0:T(8,128)(2,1)}, bf16[2,64,32,128]{3,2,1,0:T(8,128)(2,1)}, bf16[2,256,2,128]{3,2,1,0:T(2,128)(2,1)}, bf16[2,256,2,128...) custom-call(bf16[2,64,32,128]{3,2,1,0:T(8,128)(2,1)} %get-tuple-element.16.out, ...), custom_call_target="tpu_custom_call" | custom-call | tf_op jit(solution)/shard_map/pallas_call | solution.py:535
where the time goes:
time: 112 us; the launch traced here: 111 us
  Pallas kernels  111 us (99%)
    pallas_call x1, Pallas kernels, fused(): pl.pallas_call(kernel, out_shape=[jax.ShapeDtypeStruct((2, T2, 32, HD), B...  107 us
    pallas_call x1, Pallas kernels, finish(): pl.pallas_call(finish_kernel, out_shape=[rows] * 2 + [jax.ShapeDtypeStruc...  3.37 us

commit v1 on v0

--- a/solution.py
+++ b/solution.py
@@ -175,6 +175,8 @@
     py = [[mv.to(mine_1[kv], p1_of(kv), w) for kv in range(2)] for w in ys]
     ks += pass_y(zl, ky, pk_at)
     ks += pass_y(1 - zl, ky2, pk_at)
+    rs0 += pass_r(0, rx0)
+    vs += pass_y(zl, vy, pv_at)
     for cp in own_q[0] + own_p:
         cp.wait()
     got([q_in[0]] + ks)
@@ -337,6 +339,7 @@
                 for i in range(PRE // KB):
                     t = t + dot(Pm[rows, pl.ds(i * KB, KB)], prefix_rows(h, 0, prompt, i), NN)
                 dqacc[rows] = t
+            hooks[3]()
         @chunks
         def _(rc):
             rows = pl.ds(rc, RC)
@@ -427,20 +430,19 @@
 
     def resp_here():
         later["y"] = pass_z(pz, p1_at)
-        vs.extend(pass_y(zl, vy, pv_at))
-        got(rs0 + pass_r(0, rx0))
+        vs.extend(pass_y(1 - zl, vy2, pv_at))
+        got(rs0)
 
     pass_a(0, 0, resp_here)
     py2, ps = later["y"]
-    vs += pass_y(1 - zl, vy2, pv_at)
     rs1 += pass_r(1, rx1)
     got(vs)
     pass_b(0, 0, lambda: got([g_in[0]]))
     ps += pass_y(zl, py, p1_at)
+    pass_c(0, 0)
+    t00 = trade_r(0, 0)
     got(rz1)
     rx2, rs2 = spread_r(2)
-    pass_c(0, 0)
-    t00 = trade_r(0, 0)
     ps += pass_y(1 - zl, py2, p1_at)
     got(ps + rs1)
     pass_a(1, 0)
@@ -467,22 +469,24 @@
     t01 = pair_sum_r(0, 1, t01)
     pass_b(1, 1)
     swap_out(1, ob, out)
-    b0 = second(0, a0)
-    t11, a1 = [None], [None, None]
+    t11, a1, b0 = [None], [None, None], []
 
     def after_first():
         a1[0] = trade(1, 0)
-        final_r(0, 1, t01)
+        b0.extend(second(0, a0))
 
     def after_second():
         a1[1] = trade(1, 1)
         a1[0] = pair_sum(1, 0, a1[0])
+        final_r(0, 1, t01)
 
     def after_resp():
         t11[0] = trade_r(1, 1)
+
+    def after_dq():
         a1[1] = pair_sum(1, 1, a1[1])
 
-    pass_c(1, 1, (after_first, after_second, after_resp))
+    pass_c(1, 1, (after_first, after_second, after_resp, after_dq))
     swap_out(1, dqb, dout)
     t11 = pair_sum_r(1, 1, t11[0])
     final(0, b0)

time: 112 us -> 110 us (0.982)
    pallas_call x1, Pallas kernels: 107 us -> 106 us  [fused(): pl.pallas_call(kernel, out_shape=[jax.ShapeDtypeStruct((2, T2, 32, HD), B...]
where the time goes in v1:
time: 110 us
  Pallas kernels  110 us (100%)
    pallas_call x1, Pallas kernels, fused(): pl.pallas_call(kernel, out_shape=[jax.ShapeDtypeStruct((2, T2, 32, HD), B...  106 us
    pallas_call x1, Pallas kernels, finish(): pl.pallas_call(finish_kernel, out_shape=[rows] * 2 + [jax.ShapeDtypeStruc...  3.37 us

profile of v1, /device:TPU:1, one launch (start us, length us, event | category | flops | bytes accessed | tf_op | source)
XLA Modules:
  0.0 110.3 jit_solution(14237614462220725244)
XLA Ops:
  0.6 106.3 %shard_map.136 = (bf16[2,64,32,128]{3,2,1,0:T(8,128)(2,1)}, bf16[2,64,32,128]{3,2,1,0:T(8,128)(2,1)}, bf16[2,2,2,4,64,128]{5,4,3,2,1,0:T(8,128)(2,1)}, bf16[2,4,2,64,128]{4,3,2,1,0:T(8,128)(2,1)}) custom-call(s32[16]{0:T(128)} %pid.1, s32[2]{0:T(128)} %plen_ref.1, s32[16]{0:T(128)} %rlen_ref.1, bf16[2,64,32,128]{3,2,1,0:T(8,128)(2,1)} %q.1, ...), custom_call_target="tpu_custom_call" | custom-call | tf_op jit(solution)/shard_map/pallas_call | solution.py:505
  106.9 3.4 %shard_map.137 = (bf16[2,64,32,128]{3,2,1,0:T(8,128)(2,1)}, bf16[2,64,32,128]{3,2,1,0:T(8,128)(2,1)}, bf16[2,256,2,128]{3,2,1,0:T(2,128)(2,1)}, bf16[2,256,2,128...) custom-call(bf16[2,64,32,128]{3,2,1,0:T(8,128)(2,1)} %get-tuple-element.16.out, ...), custom_call_target="tpu_custom_call" | custom-call | tf_op jit(solution)/shard_map/pallas_call | solution.py:539
